TPU v7x, 32 devices: a whole 2x2x4 slice. The times are simulated.
32 devices in a mesh: replica: 2 (over core), fsdp: 16 (over z, y, x).
Axes of the slice: x: 2, y: 2, z: 4, core: 2. Of those that a mesh axis runs over, the one named last changes fastest.
Arguments:
- layer_index: int32 [2], P('replica'), may hold values from 0 to 3
- inputs: bfloat16 [8192, 4608], P(('replica', 'fsdp')), may hold values from -6 to 6
- norm_gain: float32 [4608], replicated, may hold values from 0.1 to 1.9
- cotangent: bfloat16 [8192, 1024], P(('replica', 'fsdp')), may hold values from -6 to 6
- local_fragment: bfloat16 [2, 4, 4608, 1024], P('replica', None, 'fsdp'), may hold values from -6 to 6
- global_fragment: float32 [4, 4608, 1024], P(None, 'fsdp'), may hold values from -6 to 6
- momentum: float32 [4, 4608, 1024], P(None, 'fsdp'), may hold values from -4 to 4
Outputs:
- keys_block: bfloat16 [8192, 1024], P(('replica', 'fsdp'))
- weight_grad: float32 [2, 4608, 1024], P('replica', 'fsdp')
- new_global: float32 [4, 4608, 1024], P(None, 'fsdp')
- new_momentum: float32 [4, 4608, 1024], P(None, 'fsdp')
Inputs may be any that keep to these rules, and one draw needn't show every extreme that they name: `layer_index`: a layer of the fragment for each replica.
All inputs are finite; a program needn't handle non-finite values.
Results may differ from a plain program's by a relative error of at most 0.0049.
Values may be sent and summed in bfloat16 or wider, within the bound.
A program may use at most 128 MiB of HBM per device.

v0:
```python
import jax
import jax.numpy as jnp
from jax import lax
from jax.sharding import PartitionSpec as P


def body(layer_index, inputs, norm_gain, cotangent, local_fragment, global_fragment, momentum):
    width = inputs.shape[1]
    scale_factor = float(width) ** (-0.5)
    values = inputs.astype(jnp.float32)
    stats = jnp.mean(values * values, axis=1, keepdims=True)
    normed = (values * lax.rsqrt(stats + 1e-06) * norm_gain[None, :]).astype(jnp.bfloat16)
    own_fragment = local_fragment[0]
    layer = lax.dynamic_index_in_dim(own_fragment, layer_index[0], 0, keepdims=False)
    columns = normed
    key_sum = jnp.dot(
        columns,
        lax.all_gather(layer, "fsdp", axis=0, tiled=True),
        preferred_element_type=jnp.float32,
    )
    keys_block = (key_sum * scale_factor).astype(jnp.bfloat16)
    columns = normed
    product = lax.dot_general(
        columns, cotangent, (((0,), (0,)), ((), ())), preferred_element_type=jnp.float32
    )
    grad_shard = lax.psum_scatter(product * scale_factor, "fsdp", scatter_dimension=0, tiled=True)
    weight_grad = grad_shard[None]
    delta = global_fragment - own_fragment.astype(jnp.float32)
    replicas = lax.axis_size("replica")
    average = lax.psum(delta, "replica") / replicas
    new_momentum = 0.9 * momentum + average
    new_global = global_fragment - 0.7 * (average + 0.9 * new_momentum)
    return (keys_block, weight_grad, new_global, new_momentum)


def solution(mesh):
    placed = (
        P("replica"),
        P(("replica", "fsdp"), None),
        P(),
        P(("replica", "fsdp"), None),
        P("replica", None, "fsdp", None),
        P(None, "fsdp", None),
        P(None, "fsdp", None),
    )
    return jax.shard_map(
        body,
        mesh=mesh,
        in_specs=placed,
        out_specs=(
            P(("replica", "fsdp"), None),
            P("replica", "fsdp", None),
            P(None, "fsdp", None),
            P(None, "fsdp", None),
        ),
        check_vma=False,
    )
```

profile of v0, /device:TPU:0, one launch (start us, length us, event | category | flops | bytes accessed | tf_op | source)
XLA Modules:
  0.0 439.1 jit_solution(5792875155909792293)
XLA Ops:
  8.0 0.0 copy-start
  8.0 0.0 all-reduce.2.cloned.1.call-start
  8.1 6.5 %convert_subtract_fusion = f32[4,288,1024]{2,1,0:T(8,128)} fusion(f32[4,288,1024]{2,1,0:T(8,128)} %param.12, bf16[1,4,288,1024]{3,2,1,0:T(8,128)(2,1)} %param.11), kind=kLoop, calls=%fused_computation.8 | loop fusion | flops 2359296 | bytes 11796480 | tf_op jit(solution)/shard_map/sub | solution.py:28
  14.6 0.0 copy-start.1
  14.6 0.0 copy-start.2
  14.6 0.0 all-reduce.2.cloned.1.call-update
  14.6 0.0 all-gather.3.cloned.1.call-start
  15.5 2.0 constant_dynamic-slice_fusion
  17.4 0.0 all-gather.3.cloned.1.call-update
  17.5 0.0 reduce-scatter.2.cloned.1.call-start
  17.5 0.0 copy-done.1
  17.5 0.5 fusion.2
  18.1 0.0 copy-done
  18.1 0.0 copy-done.2
  18.1 9.7 %convolution_multiply_fusion = f32[4608,1024]{1,0:T(8,128)} fusion(bf16[256,1024]{1,0:T(8,128)(2,1)S(1)} %copy-done, bf16[256,4608]{1,0:T(8,128)(2,1)S(1)} %copy-done.1, f32[4608]{0:T(1024)S(1)} %copy-done.2, f32[256]{0:T(256)S(1)} %add_rsqrt_fusion), kind=kOutput, calls=%fused_computation | convolution fusion | flops 2425356288 | bytes 21777408 | tf_op jit(solution)/shard_map/dot_general | solution.py:23
  27.8 0.0 reduce-scatter.2.cloned.1.call-update
  27.8 18.8 %all-reduce.2.cloned.1.call-done = f32[4,288,1024]{2,1,0:T(8,128)} async-done(((f32[4,288,1024]{2,1,0:T(8,128)}), f32[4,288,1024]{2,1,0:T(8,128)}) %all-reduce.2.cloned.1.call-update) | async-done | bytes 4718608 | tf_op jit(solution)/shard_map/psum | solution.py:30
  46.6 12.0 %multiply_subtract_fusion = (f32[4,288,1024]{2,1,0:T(8,128)}, f32[4,288,1024]{2,1,0:T(8,128)}) fusion(f32[4,288,1024]{2,1,0:T(8,128)} %param.12, f32[4,288,1024]{2,1,0:T(8,128)} %all-reduce.2.cloned.1.call-done, f32[4,288,1024]{2,1,0:T(8,128)} %param.13), kind=kLoop, calls=%fused_computation.9 | loop fusion | flops 8257536 | bytes 23592960 | tf_op jit(solution)/shard_map/sub | solution.py:32
  58.7 84.1 %all-gather.3.cloned.1.call-done = bf16[1,1,4608,1024]{3,2,1,0:T(8,128)(2,1)} async-done(((bf16[1,1,288,1024]{3,2,1,0:T(8,128)(2,1)}), bf16[1,1,4608,1024]{3,2,1,0:T(8,128)(2,1)}) %all-gather.3.cloned.1.call-update) | async-done | bytes 9437200 | tf_op jit(solution)/shard_map/all_gather | solution.py:18
  142.8 7.2 %fusion.8 = bf16[256,1024]{1,0:T(8,128)(2,1)} fusion(bf16[1,1,4608,1024]{3,2,1,0:T(8,128)(2,1)} %all-gather.3.cloned.1.call-done, bf16[256,4608]{1,0:T(8,128)(2,1)S(1)} %copy-done.1, f32[4608]{0:T(1024)S(1)} %copy-done.2, f32[256]{0:T(256)S(1)} %add_rsqrt_fusion), kind=kOutput, calls=%fused_computation.12 | convolution fusion | flops 2421161984 | bytes 12340224 | tf_op jit(solution)/shard_map/dot_general | solution.py:16
  149.9 281.8 %reduce-scatter.2.cloned.1.call-done = f32[288,1024]{1,0:T(8,128)} async-done(((f32[4608,1024]{1,0:T(8,128)}), f32[288,1024]{1,0:T(8,128)}) %reduce-scatter.2.cloned.1.call-update) | async-done | bytes 1179664 | tf_op jit(solution)/shard_map/reduce_scatter | solution.py:26
  (1 shorter events, 0.0 us)
Async XLA Ops:
  8.0 10.1 %copy-start = (bf16[256,1024]{1,0:T(8,128)(2,1)S(1)}, bf16[256,1024]{1,0:T(8,128)(2,1)}, u32[]{:S(2)}) copy-start(bf16[256,1024]{1,0:T(8,128)(2,1)} %param.10) | copy-start | bytes 1572868
  8.0 38.6 %all-reduce.2.cloned.1.call-start = ((), (), s32[]{:S(2)}) async-start(), calls=%async_computation.2 | async-start | bytes 9437184 | tf_op jit(solution)/shard_map/psum | solution.py:30
  14.6 2.9 copy-start.1
  14.6 3.5 copy-start.2
  14.6 128.1 %all-gather.3.cloned.1.call-start = ((), (), s32[]{:S(2)}) async-start(), calls=%async_computation.3 | async-start | bytes 10027008 | tf_op jit(solution)/shard_map/all_gather | solution.py:18
  17.5 414.2 %reduce-scatter.2.cloned.1.call-start = ((), (), s32[]{:S(2)}) async-start(), calls=%async_computation.1 | async-start | bytes 20054016 | tf_op jit(solution)/shard_map/reduce_scatter | solution.py:26
Sparse Core Ops, SparseCore 0:
  14.8 31.8 all-reduce.1
Sparse Core Ops, SparseCore 1:
  17.9 124.8 all-gather.2
  149.0 282.7 reduce-scatter.1
where the time goes:
time: 439 us
  waiting for transfers between devices  385 us (88%)
  other arithmetic  19.1 us (4%)
  matrix products  16.9 us (4%)
  between operations  16.3 us (4%)
    reduce_scatter x1, waiting for transfers between devices, body(): lax.psum_scatter(product * scale_factor, 'fsdp', scatter_dimension=0, til...  282 us
    all_gather x1, waiting for transfers between devices, body(): lax.all_gather(layer, 'fsdp', axis=0, tiled=True)  84.1 us
    psum x1, waiting for transfers between devices, body(): average = lax.psum(delta, 'replica') / replicas  18.8 us
    sub x1, other arithmetic, body(): new_global = global_fragment - 0.7 * (average + 0.9 * new_momentum)  12 us
    dot_general x1, matrix products, body(): lax.dot_general(columns, cotangent, (((0,), (0,)), ((), ())), preferred_e...  9.71 us
  transfers between devices with their start and end apart: 3, of which 3 were waited for; matrix products, arithmetic and copies ran while one was open for 7% of the time, Pallas kernels for 0%

commit v1 on v0

v1 whole, which is shorter than its diff:
```python
import functools

import jax
import jax.numpy as jnp
from jax import lax
from jax.experimental import pallas as pl
from jax.experimental.pallas import tpu as pltpu
from jax.sharding import PartitionSpec as P

INNER = 4
LANES = 128


def kernel(
    R, G, O, x_ref, gain_ref, cot_ref, w_ref, frag_in, keys_ref, grad_ref, frag_out,
    inv, nt, a, cots, ws, part, out_buf, in_buf, key_own, key_out, key_in,
    local_sem, frag_s, frag_r, cot_s, cot_r, w_s, w_r, norm_s, norm_r, key_s, key_r, sum_s, sum_r,
):
    T, D = x_ref.shape
    KV = cot_ref.shape[1]
    F = D // (G * O)
    scale = float(D) ** (-0.5)
    r = lax.axis_index("replica")
    i = lax.axis_index("fsdp")
    z, c = i // G, i % G

    def at(replica, outer, inner):
        return {"replica": replica, "fsdp": outer * G + inner}

    def remote(src, dst, send, recv, target):
        return pltpu.make_async_remote_copy(
            src_ref=src, dst_ref=dst, send_sem=send, recv_sem=recv,
            device_id=target, device_id_type=pl.DeviceIdType.MESH,
        )

    def rows(block, size):
        return pl.ds(pl.multiple_of(block * size, size), size)

    barrier = pltpu.get_barrier_semaphore()

    def greet(target):
        pl.semaphore_signal(barrier, inc=1, device_id=target, device_id_type=pl.DeviceIdType.MESH)

    for k in range(1, G):
        greet(at(r, z, (c + k) % G))
    for k in range(1, R):
        greet(at((r + k) % R, z, c))
    has_left, has_right = z > 0, z < O - 1

    @pl.when(has_left)
    def _():
        greet(at(r, z - 1, c))

    @pl.when(has_right)
    def _():
        greet(at(r, z + 1, c))

    pl.semaphore_wait(barrier, G - 1 + R - 1 + jnp.where(has_left, 1, 0) + jnp.where(has_right, 1, 0))

    def cot_copy(k):
        return remote(cot_ref, cots.at[rows(c, T)], cot_s.at[k], cot_r.at[k], at(r, z, (c + k) % G))

    def frag_copy(k):
        return remote(frag_in, frag_out.at[r], frag_s.at[k], frag_r.at[k], at((r + k) % R, z, c))

    def w_copy(side, hop):
        block = z - (hop - 1) if side == 0 else z + (hop - 1)
        where = ws.at[rows(block, F)]
        return remote(
            w_ref if hop == 1 else where, where, w_s.at[side, hop], w_r.at[side, hop],
            at(r, z + 1 if side == 0 else z - 1, c),
        )

    def w_sends(side, hop):
        if side == 0:
            return jnp.logical_and(z >= hop - 1, z < O - 1)
        return jnp.logical_and(z + hop - 1 <= O - 1, z > 0)

    def w_comes(side, hop):
        return z >= hop if side == 0 else z + hop <= O - 1

    def w_start(hop):
        for side in range(2):
            @pl.when(w_sends(side, hop))
            def _(side=side):
                w_copy(side, hop).start()

    def w_wait(hop):
        for side in range(2):
            @pl.when(w_comes(side, hop))
            def _(side=side):
                block = z - hop if side == 0 else z + hop
                where = ws.at[rows(block, F)]
                remote(where, where, w_s.at[side, hop], w_r.at[side, hop], at(r, z, (c + 1) % G)).wait_recv()

    for k in range(1, G):
        cot_copy(k).start()
    w_start(1)
    for k in range(1, R):
        frag_copy(k).start()
    mine = [
        pltpu.make_async_copy(cot_ref, cots.at[rows(c, T)], local_sem.at[0]),
        pltpu.make_async_copy(w_ref, ws.at[rows(z, F)], local_sem.at[1]),
        pltpu.make_async_copy(frag_in, frag_out.at[r], local_sem.at[2]),
    ]
    for copy in mine:
        copy.start()

    step = 16

    @pl.loop(0, T // step)
    def _(t):
        here = pl.ds(pl.multiple_of(t * step, step), step)
        values = x_ref[here, :].astype(jnp.float32)
        stats = jnp.mean(values * values, axis=1, keepdims=True)
        inv[here, :] = jnp.broadcast_to(lax.rsqrt(stats + 1e-06), (step, LANES))

    def transpose_chunks(start, count):
        @pl.loop(0, count)
        def _(j):
            here = pl.ds(pl.multiple_of(start + j * LANES, LANES), LANES)
            normed = x_ref[:, here].astype(jnp.float32) * inv[...] * gain_ref[:, here]
            nt[here, :] = normed.T.astype(jnp.bfloat16)

    def order(k):
        far = O - 1 - k // 2 if k % 2 == 0 else k // 2
        return jnp.where(z < O // 2, far, O - 1 - far)

    def norm_copy(d, k):
        peer = (c + k) % G
        return remote(
            nt.at[rows(d * G + peer, F)],
            a.at[rows(d, F), rows(c, T)],
            norm_s.at[d, k], norm_r.at[d, k], at(r, z, peer),
        )

    whole = (G * F) % LANES != 0
    if whole:
        transpose_chunks(0, D // LANES)
    for n in range(O):
        d = order(n)
        if not whole:
            transpose_chunks(d * (G * F), G * F // LANES)
        for k in range(1, G):
            norm_copy(d, k).start()
        a[rows(d, F), rows(c, T)] = nt[rows(d * G + c, F), :]

    def sum_copy(d):
        side = jnp.where(z < d, 0, 1)
        return remote(
            out_buf.at[d], in_buf.at[side, d], sum_s.at[d], sum_r.at[side, d],
            at(r, jnp.where(z < d, z + 1, z - 1), c),
        )

    def sum_wait(side, d):
        where = in_buf.at[side, d]
        remote(where, where, sum_s.at[d], sum_r.at[side, d], at(r, z, (c + 1) % G)).wait_recv()

    tile = min(512, KV)
    for n in range(O):
        d = order(n)
        if n + 1 < O:
            w_wait(n + 1)
            if n + 2 < O:
                w_start(n + 2)
        if n == 0:
            for copy in mine:
                copy.wait()
            for k in range(1, G):
                cot_copy(k).wait_recv()
        for k in range(1, G):
            norm_copy(d, k).wait_recv()
        for m in range(KV // tile):
            cols = pl.ds(m * tile, tile)
            part[d, :, cols] = jnp.dot(a[rows(d, F), :], cots[:, cols], preferred_element_type=jnp.float32)
        first = jnp.logical_or(jnp.logical_and(z == 0, d > 0), jnp.logical_and(z == O - 1, d < O - 1))

        @pl.when(first)
        def _(d=d):
            out_buf[d] = part[d].astype(jnp.bfloat16)
            sum_copy(d).start()

    def key_copy(k):
        return remote(key_out.at[k], key_in.at[k], key_s.at[k], key_r.at[k], at(r, z, (c + k) % G))

    for k in list(range(1, G)) + [0]:
        tokens = rows((c + k) % G, T)
        for m in range(KV // tile):
            cols = pl.ds(m * tile, tile)
            term = lax.dot_general(
                a[:, tokens], ws[:, cols], (((0,), (0,)), ((), ())), preferred_element_type=jnp.float32
            )
            if k:
                key_out[k, :, cols] = term.astype(jnp.bfloat16)
            else:
                key_own[:, cols] = term
        if k:
            key_copy(k).start()

    for n in range(O):
        d = order(n)
        between = jnp.logical_and(d != z, jnp.logical_and(z > 0, z < O - 1))

        @pl.when(between)
        def _(d=d):
            side = jnp.where(z < d, 0, 1)
            sum_wait(side, d)
            out_buf[d] = (part[d] + in_buf[side, d].astype(jnp.float32)).astype(jnp.bfloat16)
            sum_copy(d).start()

    grad_ref[...] = part[z]

    @pl.when(has_left)
    def _():
        sum_wait(0, z)
        grad_ref[...] += in_buf[0, z].astype(jnp.float32)

    @pl.when(has_right)
    def _():
        sum_wait(1, z)
        grad_ref[...] += in_buf[1, z].astype(jnp.float32)

    grad_ref[...] = grad_ref[...] * scale

    for k in range(1, G):
        key_copy(k).wait_recv()
    total = key_own[...]
    for k in range(1, G):
        total = total + key_in[k].astype(jnp.float32)
    keys_ref[...] = (total * scale).astype(jnp.bfloat16)

    for k in range(1, R):
        frag_copy(k).wait()
    for k in range(1, G):
        cot_copy(k).wait_send()
        key_copy(k).wait_send()
    for d in range(O):
        for k in range(1, G):
            norm_copy(d, k).wait_send()

        @pl.when(z != d)
        def _(d=d):
            sum_copy(d).wait_send()
    for hop in range(1, O):
        for side in range(2):
            @pl.when(w_sends(side, hop))
            def _(side=side, hop=hop):
                w_copy(side, hop).wait_send()


def body(layer_index, inputs, norm_gain, cotangent, local_fragment, global_fragment, momentum):
    R, S = lax.axis_size("replica"), lax.axis_size("fsdp")
    G = INNER
    O = S // G
    T, D = inputs.shape
    KV = cotangent.shape[1]
    F = D // S
    own = local_fragment[0]
    layer = lax.dynamic_index_in_dim(own, layer_index[0], 0, keepdims=False)
    bf16, f32 = jnp.bfloat16, jnp.float32
    vmem, anywhere = pl.BlockSpec(memory_space=pltpu.VMEM), pl.BlockSpec(memory_space=pl.ANY)
    dma = pltpu.SemaphoreType.DMA
    keys_block, grad, fragments = pl.pallas_call(
        functools.partial(kernel, R, G, O),
        out_shape=(
            jax.ShapeDtypeStruct((T, KV), bf16),
            jax.ShapeDtypeStruct((F, KV), f32),
            jax.ShapeDtypeStruct((R,) + own.shape, bf16),
        ),
        in_specs=[vmem, vmem, anywhere, anywhere, anywhere],
        out_specs=(vmem, vmem, anywhere),
        scratch_shapes=[
            pltpu.VMEM((T, LANES), f32),
            pltpu.VMEM((D, T), bf16),
            pltpu.VMEM((O * F, G * T), bf16),
            pltpu.VMEM((G * T, KV), bf16),
            pltpu.VMEM((O * F, KV), bf16),
            pltpu.VMEM((O, F, KV), f32),
            pltpu.VMEM((O, F, KV), bf16),
            pltpu.VMEM((2, O, F, KV), bf16),
            pltpu.VMEM((T, KV), f32),
            pltpu.VMEM((G, T, KV), bf16),
            pltpu.VMEM((G, T, KV), bf16),
            dma((3,)), dma((R,)), dma((R,)), dma((G,)), dma((G,)),
            dma((2, O)), dma((2, O)), dma((O, G)), dma((O, G)),
            dma((G,)), dma((G,)), dma((O,)), dma((2, O)),
        ],
        compiler_params=pltpu.CompilerParams(
            collective_id=0, has_side_effects=True, vmem_limit_bytes=56 * 1024 * 1024
        ),
        cost_estimate=pl.CostEstimate(flops=4 * T * D * KV, bytes_accessed=16 * 1024 * 1024, transcendentals=T),
    )(inputs, norm_gain[None, :], cotangent, layer, own)
    weight_grad = grad[None]
    total = global_fragment - fragments[0].astype(f32)
    for k in range(1, R):
        total = total + (global_fragment - fragments[k].astype(f32))
    average = total / R
    new_momentum = 0.9 * momentum + average
    new_global = global_fragment - 0.7 * (average + 0.9 * new_momentum)
    return (keys_block, weight_grad, new_global, new_momentum)


def solution(mesh):
    placed = (
        P("replica"),
        P(("replica", "fsdp"), None),
        P(),
        P(("replica", "fsdp"), None),
        P("replica", None, "fsdp", None),
        P(None, "fsdp", None),
        P(None, "fsdp", None),
    )
    return jax.shard_map(
        body,
        mesh=mesh,
        in_specs=placed,
        out_specs=(
            P(("replica", "fsdp"), None),
            P("replica", "fsdp", None),
            P(None, "fsdp", None),
            P(None, "fsdp", None),
        ),
        check_vma=False,
    )
```

time: 439 us -> 138 us (0.31)
  waiting for transfers between devices: 385 us -> 0 us
  Pallas kernels: 0 us -> 124 us
  matrix products: 16.9 us -> 0 us
  between operations: 16.3 us -> 1.33 us
  other arithmetic: 19.1 us -> 7.41 us
    reduce_scatter x1 -> x0, waiting for transfers between devices: 282 us -> none  [body(): lax.psum_scatter(product * scale_factor, 'fsdp', scatter_dimension=0, til...]
    pallas_call x0 -> x1, Pallas kernels: none -> 124 us  [body(): pl.pallas_call(functools.partial(kernel, R, G, O), out_shape=(jax.ShapeDt...]
    all_gather x1 -> x0, waiting for transfers between devices: 84.1 us -> none  [body(): lax.all_gather(layer, 'fsdp', axis=0, tiled=True)]
    psum x1 -> x0, waiting for transfers between devices: 18.8 us -> none  [body(): average = lax.psum(delta, 'replica') / replicas]
    dot_general x2 -> x0, matrix products: 16.9 us -> none  [the longest x1 9.71 us: body(): lax.dot_general(columns, cotangent, (((0,), (0,)), ((), ())), preferred_e...]
    sub x1 -> x0, other arithmetic: 6.54 us -> none  [body(): delta = global_fragment - own_fragment.astype(jnp.float32)]
    sub x1, other arithmetic: 12 us -> 7.41 us  [body(): new_global = global_fragment - 0.7 * (average + 0.9 * new_momentum)]
  transfers between devices with their start and end apart: 3 -> 0, of which waited for: 3 -> 0; matrix products, arithmetic and copies ran while one was open for 7% -> 0% of each run, Pallas kernels for 0% -> 0%
where the time goes in v1:
time: 138 us
  Pallas kernels  124 us (90%)
  other arithmetic  7.41 us (5%)
  local copies, waits for them, and re-layouts  5.23 us (4%)
    pallas_call x1, Pallas kernels, body(): pl.pallas_call(functools.partial(kernel, R, G, O), out_shape=(jax.ShapeDt...  124 us
    sub x1, other arithmetic, body(): new_global = global_fragment - 0.7 * (average + 0.9 * new_momentum)  7.41 us

profile of v1, /device:TPU:0, one launch (start us, length us, event | category | flops | bytes accessed | tf_op | source)
XLA Modules:
  0.0 137.7 jit_solution(17540576680771901924)
XLA Ops:
  1.3 1.3 broadcast_in_dim.6.gain_ref
  2.6 0.0 slice-start
  2.6 2.1 %dynamic-slice_bitcast_fusion.w_ref = bf16[288,1024]{1,0:T(8,128)(2,1)} fusion(bf16[1,4,288,1024]{3,2,1,0:T(8,128)(2,1)} %param.11, s32[]{:T(128)S(6)} %select_n.4), kind=kLoop, calls=%fused_computation.6 | loop fusion | bytes 1179652 | tf_op jit(solution)/shard_map/jit(dynamic_index_in_dim)/squeeze | solution.py:259
  4.7 0.0 slice-start.1
  4.7 123.7 %shard_map.102 = (bf16[256,1024]{1,0:T(8,128)(2,1)}, f32[288,1024]{1,0:T(8,128)}, bf16[2,4,288,1024]{3,2,1,0:T(8,128)(2,1)}) custom-call(bf16[256,4608]{1,0:T(8,128)(2,1)} %x_ref.1, f32[1,4608]{1,0:T(1,128)} %broadcast_in_dim.6.gain_ref, bf16[256,1024]{1,0:T(8,128)(2,1)} %cot_ref.1, bf16[288,1024]{1,0:T(8,128)(2,1)} %dynamic-slice_bitcast_fusion.w_ref, ...), custom_call_target="tpu_custom_call" | custom-call | flops 4831838208 | bytes 16777216 | tf_op jit(solution)/shard_map/pallas_call | solution.py:263
  128.4 0.0 slice-done
  128.4 0.0 slice-done.1
  128.4 0.0 copy-start.1
  128.5 0.0 copy-start
  128.5 7.4 %multiply_subtract_fusion = (f32[4,288,1024]{2,1,0:T(8,128)}, f32[4,288,1024]{2,1,0:T(8,128)}) fusion(f32[4,288,1024]{2,1,0:T(8,128)S(1)} %bitcast.22, bf16[2,4,288,1024]{3,2,1,0:T(8,128)(2,1)} %get-tuple-element.9, f32[4,288,1024]{2,1,0:T(8,128)} %param.13), kind=kLoop, calls=%fused_computation.4 | loop fusion | flops 14155776 | bytes 23592960 | tf_op jit(solution)/shard_map/sub | solution.py:299
  135.9 0.0 copy-done.1
  135.9 0.8 copy.14
  136.7 0.0 copy-done
  136.7 1.0 copy.15
  (1 shorter events, 0.0 us)
Async XLA Ops:
  2.6 125.8 %slice-start = ((s8[4718592]{0:T(1024)(128)(4,1)}), s8[4194304]{0:T(1024)(128)(4,1)S(1)}, s32[]{:S(2)}) async-start(s8[4718592]{0:T(1024)(128)(4,1)} %bitcast.21), calls=%async_computation | async-start | bytes 8388608
  4.7 123.7 %slice-start.1 = ((s8[4718592]{0:T(1024)(128)(4,1)}), s8[524288]{0:T(1024)(128)(4,1)S(1)}, s32[]{:S(2)}) async-start(s8[4718592]{0:T(1024)(128)(4,1)} %bitcast.21), calls=%async_computation.1 | async-start | bytes 1048576
  128.4 7.4 %copy-start.1 = (bf16[256,1024]{1,0:T(8,128)(2,1)S(1)}, bf16[256,1024]{1,0:T(8,128)(2,1)}, u32[]{:S(2)}) copy-start(bf16[256,1024]{1,0:T(8,128)(2,1)} %get-tuple-element.16) | copy-start | bytes 1572868
  128.5 8.2 %copy-start = (f32[288,1024]{1,0:T(8,128)S(1)}, f32[288,1024]{1,0:T(8,128)}, u32[]{:S(2)}) copy-start(f32[288,1024]{1,0:T(8,128)} %get-tuple-element.8) | copy-start | bytes 3538948

commit v2 on v1

--- a/solution.py
+++ b/solution.py
@@ -12,8 +12,8 @@
 
 
 def kernel(
-    R, G, O, x_ref, gain_ref, cot_ref, w_ref, frag_in, keys_ref, grad_ref, frag_out,
-    inv, nt, a, cots, ws, part, out_buf, in_buf, key_own, key_out, key_in,
+    R, G, O, pick_ref, x_ref, gain_ref, cot_ref, frag_in, keys_ref, grad_ref, frag_out,
+    inv, nt, a, cots, ws, part, out_buf, in_buf, key_own, key_add, key_out, key_in,
     local_sem, frag_s, frag_r, cot_s, cot_r, w_s, w_r, norm_s, norm_r, key_s, key_r, sum_s, sum_r,
 ):
     T, D = x_ref.shape
@@ -23,6 +23,8 @@
     r = lax.axis_index("replica")
     i = lax.axis_index("fsdp")
     z, c = i // G, i % G
+    cx, cy = c % 2, c // 2
+    plane = [c, cy * 2 + 1 - cx, (1 - cy) * 2 + cx, 3 - c]
 
     def at(replica, outer, inner):
         return {"replica": replica, "fsdp": outer * G + inner}
@@ -42,7 +44,7 @@
         pl.semaphore_signal(barrier, inc=1, device_id=target, device_id_type=pl.DeviceIdType.MESH)
 
     for k in range(1, G):
-        greet(at(r, z, (c + k) % G))
+        greet(at(r, z, plane[k]))
     for k in range(1, R):
         greet(at((r + k) % R, z, c))
     has_left, has_right = z > 0, z < O - 1
@@ -57,8 +59,18 @@
 
     pl.semaphore_wait(barrier, G - 1 + R - 1 + jnp.where(has_left, 1, 0) + jnp.where(has_right, 1, 0))
 
+    half = T // 2
+
     def cot_copy(k):
-        return remote(cot_ref, cots.at[rows(c, T)], cot_s.at[k], cot_r.at[k], at(r, z, (c + k) % G))
+        return remote(cot_ref, cots.at[rows(c, T)], cot_s.at[k], cot_r.at[k], at(r, z, plane[k]))
+
+    def cot_pass(k):
+        where = cots.at[pl.ds(pl.multiple_of(plane[k] * T + (k - 1) * half, half), half)]
+        return remote(where, where, cot_s.at[2 + k], cot_r.at[2 + k], at(r, z, plane[3 - k]))
+
+    def cot_passed(k):
+        where = cots.at[pl.ds(pl.multiple_of(plane[3] * T + (2 - k) * half, half), half)]
+        return remote(where, where, cot_s.at[5 - k], cot_r.at[5 - k], at(r, z, plane[k]))
 
     def frag_copy(k):
         return remote(frag_in, frag_out.at[r], frag_s.at[k], frag_r.at[k], at((r + k) % R, z, c))
@@ -67,7 +79,7 @@
         block = z - (hop - 1) if side == 0 else z + (hop - 1)
         where = ws.at[rows(block, F)]
         return remote(
-            w_ref if hop == 1 else where, where, w_s.at[side, hop], w_r.at[side, hop],
+            where, where, w_s.at[side, hop], w_r.at[side, hop],
             at(r, z + 1 if side == 0 else z - 1, c),
         )
 
@@ -91,17 +103,15 @@
             def _(side=side):
                 block = z - hop if side == 0 else z + hop
                 where = ws.at[rows(block, F)]
-                remote(where, where, w_s.at[side, hop], w_r.at[side, hop], at(r, z, (c + 1) % G)).wait_recv()
-
-    for k in range(1, G):
+                remote(where, where, w_s.at[side, hop], w_r.at[side, hop], at(r, z, plane[1])).wait_recv()
+
+    for k in (1, 2):
         cot_copy(k).start()
+    ws[rows(z, F), :] = frag_in[pick_ref[0]]
     w_start(1)
-    for k in range(1, R):
-        frag_copy(k).start()
     mine = [
         pltpu.make_async_copy(cot_ref, cots.at[rows(c, T)], local_sem.at[0]),
-        pltpu.make_async_copy(w_ref, ws.at[rows(z, F)], local_sem.at[1]),
-        pltpu.make_async_copy(frag_in, frag_out.at[r], local_sem.at[2]),
+        pltpu.make_async_copy(frag_in, frag_out.at[r], local_sem.at[1]),
     ]
     for copy in mine:
         copy.start()
@@ -127,7 +137,7 @@
         return jnp.where(z < O // 2, far, O - 1 - far)
 
     def norm_copy(d, k):
-        peer = (c + k) % G
+        peer = plane[k]
         return remote(
             nt.at[rows(d * G + peer, F)],
             a.at[rows(d, F), rows(c, T)],
@@ -144,6 +154,12 @@
         for k in range(1, G):
             norm_copy(d, k).start()
         a[rows(d, F), rows(c, T)] = nt[rows(d * G + c, F), :]
+        if n == min(1, O - 1):
+            for k in (1, 2):
+                cot_copy(k).wait_recv()
+                cot_pass(k).start()
+    for k in range(1, R):
+        frag_copy(k).start()
 
     def sum_copy(d):
         side = jnp.where(z < d, 0, 1)
@@ -154,7 +170,17 @@
 
     def sum_wait(side, d):
         where = in_buf.at[side, d]
-        remote(where, where, sum_s.at[d], sum_r.at[side, d], at(r, z, (c + 1) % G)).wait_recv()
+        remote(where, where, sum_s.at[d], sum_r.at[side, d], at(r, z, plane[1])).wait_recv()
+
+    def pass_on(d):
+        between = jnp.logical_and(d != z, jnp.logical_and(z > 0, z < O - 1))
+
+        @pl.when(between)
+        def _():
+            side = jnp.where(z < d, 0, 1)
+            sum_wait(side, d)
+            out_buf[d] = (part[d] + in_buf[side, d].astype(jnp.float32)).astype(jnp.bfloat16)
+            sum_copy(d).start()
 
     tile = min(512, KV)
     for n in range(O):
@@ -166,8 +192,8 @@
         if n == 0:
             for copy in mine:
                 copy.wait()
-            for k in range(1, G):
-                cot_copy(k).wait_recv()
+            for k in (1, 2):
+                cot_passed(k).wait_recv()
         for k in range(1, G):
             norm_copy(d, k).wait_recv()
         for m in range(KV // tile):
@@ -180,33 +206,62 @@
             out_buf[d] = part[d].astype(jnp.bfloat16)
             sum_copy(d).start()
 
-    def key_copy(k):
-        return remote(key_out.at[k], key_in.at[k], key_s.at[k], key_r.at[k], at(r, z, (c + k) % G))
-
-    for k in list(range(1, G)) + [0]:
-        tokens = rows((c + k) % G, T)
+        if n == O - 2:
+            pass_on(order(0))
+
+    top, bottom = pl.ds(0, half), pl.ds(half, half)
+
+    def key_term(k, put):
+        tokens = rows(plane[k], T)
         for m in range(KV // tile):
             cols = pl.ds(m * tile, tile)
-            term = lax.dot_general(
+            put(cols, lax.dot_general(
                 a[:, tokens], ws[:, cols], (((0,), (0,)), ((), ())), preferred_element_type=jnp.float32
-            )
-            if k:
-                key_out[k, :, cols] = term.astype(jnp.bfloat16)
-            else:
-                key_own[:, cols] = term
-        if k:
-            key_copy(k).start()
-
-    for n in range(O):
-        d = order(n)
-        between = jnp.logical_and(d != z, jnp.logical_and(z > 0, z < O - 1))
-
-        @pl.when(between)
-        def _(d=d):
-            side = jnp.where(z < d, 0, 1)
-            sum_wait(side, d)
-            out_buf[d] = (part[d] + in_buf[side, d].astype(jnp.float32)).astype(jnp.bfloat16)
-            sum_copy(d).start()
+            ))
+
+    def key_copy(k, part_of, slot, target):
+        return remote(
+            key_out.at[k, part_of], key_in.at[k, part_of], key_s.at[slot], key_r.at[slot], at(r, z, target)
+        )
+
+    across = [key_copy(3, top, 0, plane[1]), key_copy(3, bottom, 1, plane[2])]
+    plain = [key_copy(1, top, 2, plane[1]), key_copy(2, bottom, 3, plane[2])]
+    summed = [key_copy(1, bottom, 4, plane[1]), key_copy(2, top, 5, plane[2])]
+
+    def put_across(cols, term):
+        key_out[3, :, cols] = term.astype(jnp.bfloat16)
+
+    key_term(3, put_across)
+    for copy in across:
+        copy.start()
+
+    def put_x(cols, term):
+        key_out[1, top, cols] = term[:half].astype(jnp.bfloat16)
+        key_add[0, :, cols] = term[half:]
+
+    key_term(1, put_x)
+    plain[0].start()
+
+    def put_y(cols, term):
+        key_out[2, bottom, cols] = term[half:].astype(jnp.bfloat16)
+        key_add[1, :, cols] = term[:half]
+
+    key_term(2, put_y)
+    plain[1].start()
+
+    def put_own(cols, term):
+        key_own[:, cols] = term
+
+    key_term(0, put_own)
+    across[1].wait_recv()
+    key_out[1, bottom, :] = (key_add[0] + key_in[3, bottom, :].astype(jnp.float32)).astype(jnp.bfloat16)
+    summed[0].start()
+    across[0].wait_recv()
+    key_out[2, top, :] = (key_add[1] + key_in[3, top, :].astype(jnp.float32)).astype(jnp.bfloat16)
+    summed[1].start()
+
+    for n in range(1, O):
+        pass_on(order(n))
 
     grad_ref[...] = part[z]
 
@@ -222,18 +277,18 @@
 
     grad_ref[...] = grad_ref[...] * scale
 
-    for k in range(1, G):
-        key_copy(k).wait_recv()
-    total = key_own[...]
-    for k in range(1, G):
-        total = total + key_in[k].astype(jnp.float32)
+    for copy in plain + summed:
+        copy.wait_recv()
+    total = key_own[...] + key_in[1].astype(jnp.float32) + key_in[2].astype(jnp.float32)
     keys_ref[...] = (total * scale).astype(jnp.bfloat16)
 
     for k in range(1, R):
         frag_copy(k).wait()
-    for k in range(1, G):
+    for copy in across + plain + summed:
+        copy.wait_send()
+    for k in (1, 2):
         cot_copy(k).wait_send()
-        key_copy(k).wait_send()
+        cot_pass(k).wait_send()
     for d in range(O):
         for k in range(1, G):
             norm_copy(d, k).wait_send()
@@ -256,7 +311,6 @@
     KV = cotangent.shape[1]
     F = D // S
     own = local_fragment[0]
-    layer = lax.dynamic_index_in_dim(own, layer_index[0], 0, keepdims=False)
     bf16, f32 = jnp.bfloat16, jnp.float32
     vmem, anywhere = pl.BlockSpec(memory_space=pltpu.VMEM), pl.BlockSpec(memory_space=pl.ANY)
     dma = pltpu.SemaphoreType.DMA
@@ -267,7 +321,7 @@
             jax.ShapeDtypeStruct((F, KV), f32),
             jax.ShapeDtypeStruct((R,) + own.shape, bf16),
         ),
-        in_specs=[vmem, vmem, anywhere, anywhere, anywhere],
+        in_specs=[pl.BlockSpec(memory_space=pltpu.SMEM), vmem, vmem, vmem, vmem],
         out_specs=(vmem, vmem, anywhere),
         scratch_shapes=[
             pltpu.VMEM((T, LANES), f32),
@@ -279,17 +333,18 @@
             pltpu.VMEM((O, F, KV), bf16),
             pltpu.VMEM((2, O, F, KV), bf16),
             pltpu.VMEM((T, KV), f32),
+            pltpu.VMEM((2, T // 2, KV), f32),
             pltpu.VMEM((G, T, KV), bf16),
             pltpu.VMEM((G, T, KV), bf16),
-            dma((3,)), dma((R,)), dma((R,)), dma((G,)), dma((G,)),
+            dma((2,)), dma((R,)), dma((R,)), dma((5,)), dma((5,)),
             dma((2, O)), dma((2, O)), dma((O, G)), dma((O, G)),
-            dma((G,)), dma((G,)), dma((O,)), dma((2, O)),
+            dma((6,)), dma((6,)), dma((O,)), dma((2, O)),
         ],
         compiler_params=pltpu.CompilerParams(
             collective_id=0, has_side_effects=True, vmem_limit_bytes=56 * 1024 * 1024
         ),
         cost_estimate=pl.CostEstimate(flops=4 * T * D * KV, bytes_accessed=16 * 1024 * 1024, transcendentals=T),
-    )(inputs, norm_gain[None, :], cotangent, layer, own)
+    )(layer_index, inputs, norm_gain[None, :], cotangent, own)
     weight_grad = grad[None]
     total = global_fragment - fragments[0].astype(f32)
     for k in range(1, R):

time: 138 us -> 90.2 us (0.65)
  Pallas kernels: 124 us -> 77.8 us
  local copies, waits for them, and re-layouts: 5.23 us -> 3.17 us
    pallas_call x1, Pallas kernels: 124 us -> 77.8 us  [body(): pl.pallas_call(functools.partial(kernel, R, G, O), out_shape=(jax.ShapeDt...]
    squeeze x1 -> x0, local copies, waits for them, and re-layouts: 2.07 us -> none  [body(): layer = lax.dynamic_index_in_dim(own, layer_index[0], 0, keepdims=False)]
where the time goes in v2:
time: 90.2 us; the launch traced here: 89.7 us
  Pallas kernels  77.8 us (86%)
  other arithmetic  7.41 us (8%)
  local copies, waits for them, and re-layouts  3.17 us (4%)
  between operations  1.31 us (1%)
    pallas_call x1, Pallas kernels, body(): pl.pallas_call(functools.partial(kernel, R, G, O), out_shape=(jax.ShapeDt...  77.8 us
    sub x1, other arithmetic, body(): new_global = global_fragment - 0.7 * (average + 0.9 * new_momentum)  7.41 us
    unnamed x8, local copies, waits for them, and re-layouts  1.82 us

profile of v2, /device:TPU:0, one launch (start us, length us, event | category | flops | bytes accessed | tf_op | source)
XLA Modules:
  0.0 89.7 jit_solution(2559728563284460755)
XLA Ops:
  1.3 1.3 %broadcast_in_dim.6.gain_ref = f32[1,4608]{1,0:T(1,128)} reshape(f32[4608]{0:T(1024)} %param.9) | data formatting | bytes 36864 | tf_op jit(solution)/shard_map/broadcast_in_dim | solution.py:347
  2.6 0.0 copy-start
  2.6 77.8 %shard_map.102 = (bf16[256,1024]{1,0:T(8,128)(2,1)}, f32[288,1024]{1,0:T(8,128)}, bf16[2,4,288,1024]{3,2,1,0:T(8,128)(2,1)}) custom-call(s32[1]{0:T(128)S(6)} %copy.13.pick_ref, bf16[256,4608]{1,0:T(8,128)(2,1)} %x_ref.1, f32[1,4608]{1,0:T(1,128)} %broadcast_in_dim.6.gain_ref, bf16[256,1024]{1,0:T(8,128)(2,1)} %cot_ref.1, bf16[4,288,1024]{2,1,0:T(8,128)(2,1)} %bitcast.16), custom_call_target="tpu_custom_call" | custom-call | flops 4831838208 | bytes 16777216 | tf_op jit(solution)/shard_map/pallas_call | solution.py:317
  80.4 0.0 copy-done
  80.4 0.0 copy-start.2
  80.4 0.0 copy-start.1
  80.4 7.4 %multiply_subtract_fusion = (f32[4,288,1024]{2,1,0:T(8,128)}, f32[4,288,1024]{2,1,0:T(8,128)}) fusion(f32[4,288,1024]{2,1,0:T(8,128)S(1)} %copy-done, bf16[2,4,288,1024]{3,2,1,0:T(8,128)(2,1)} %get-tuple-element.9, f32[4,288,1024]{2,1,0:T(8,128)} %param.13), kind=kLoop, calls=%fused_computation.4 | loop fusion | flops 14155776 | bytes 23592960 | tf_op jit(solution)/shard_map/sub | solution.py:354
  87.8 0.0 copy-done.2
  87.8 0.8 copy.14
  88.6 0.0 copy-done.1
  88.6 1.0 %copy.15 = f32[1,288,1024]{2,1,0:T(8,128)} copy(f32[1,288,1024]{2,1,0:T(8,128)S(1)} %bitcast.15) | data formatting | bytes 2359296
Async XLA Ops:
  2.6 77.8 %copy-start = (f32[4,288,1024]{2,1,0:T(8,128)S(1)}, f32[4,288,1024]{2,1,0:T(8,128)}, u32[]{:S(2)}) copy-start(f32[4,288,1024]{2,1,0:T(8,128)} %param.12) | copy-start | bytes 14155780
  80.4 7.4 %copy-start.2 = (bf16[256,1024]{1,0:T(8,128)(2,1)S(1)}, bf16[256,1024]{1,0:T(8,128)(2,1)}, u32[]{:S(2)}) copy-start(bf16[256,1024]{1,0:T(8,128)(2,1)} %get-tuple-element.16) | copy-start | bytes 1572868
  80.4 8.2 %copy-start.1 = (f32[288,1024]{1,0:T(8,128)S(1)}, f32[288,1024]{1,0:T(8,128)}, u32[]{:S(2)}) copy-start(f32[288,1024]{1,0:T(8,128)} %get-tuple-element.8) | copy-start | bytes 3538948

commit v3 on v2

--- a/solution.py
+++ b/solution.py
@@ -12,8 +12,8 @@
 
 
 def kernel(
-    R, G, O, pick_ref, x_ref, gain_ref, cot_ref, frag_in, keys_ref, grad_ref, frag_out,
-    inv, nt, a, cots, ws, part, out_buf, in_buf, key_own, key_add, key_out, key_in,
+    R, G, O, pick_ref, x_hbm, gain_ref, cot_ref, frag_hbm, keys_ref, grad_ref, frag_out,
+    x_ref, frag_in, inv, nt, a, cots, ws, part, out_buf, in_buf, key_own, key_add, key_out, key_in,
     local_sem, frag_s, frag_r, cot_s, cot_r, w_s, w_r, norm_s, norm_r, key_s, key_r, sum_s, sum_r,
 ):
     T, D = x_ref.shape
@@ -38,6 +38,11 @@
     def rows(block, size):
         return pl.ds(pl.multiple_of(block * size, size), size)
 
+    load_x = pltpu.make_async_copy(x_hbm, x_ref, local_sem.at[2])
+    load_frag = pltpu.make_async_copy(frag_hbm, frag_in, local_sem.at[3])
+    load_frag.start()
+    load_x.start()
+
     barrier = pltpu.get_barrier_semaphore()
 
     def greet(target):
@@ -107,6 +112,7 @@
 
     for k in (1, 2):
         cot_copy(k).start()
+    load_frag.wait()
     ws[rows(z, F), :] = frag_in[pick_ref[0]]
     w_start(1)
     mine = [
@@ -116,6 +122,7 @@
     for copy in mine:
         copy.start()
 
+    load_x.wait()
     step = 16
 
     @pl.loop(0, T // step)
@@ -129,7 +136,7 @@
         @pl.loop(0, count)
         def _(j):
             here = pl.ds(pl.multiple_of(start + j * LANES, LANES), LANES)
-            normed = x_ref[:, here].astype(jnp.float32) * inv[...] * gain_ref[:, here]
+            normed = x_ref[:, here].astype(jnp.float32) * inv[...] * gain_ref[here][None, :]
             nt[here, :] = normed.T.astype(jnp.bfloat16)
 
     def order(k):
@@ -154,10 +161,13 @@
         for k in range(1, G):
             norm_copy(d, k).start()
         a[rows(d, F), rows(c, T)] = nt[rows(d * G + c, F), :]
-        if n == min(1, O - 1):
+        if n == 0:
             for k in (1, 2):
                 cot_copy(k).wait_recv()
                 cot_pass(k).start()
+            w_wait(1)
+            if O > 2:
+                w_start(2)
     for k in range(1, R):
         frag_copy(k).start()
 
@@ -185,7 +195,7 @@
     tile = min(512, KV)
     for n in range(O):
         d = order(n)
-        if n + 1 < O:
+        if n and n + 1 < O:
             w_wait(n + 1)
             if n + 2 < O:
                 w_start(n + 2)
@@ -321,9 +331,11 @@
             jax.ShapeDtypeStruct((F, KV), f32),
             jax.ShapeDtypeStruct((R,) + own.shape, bf16),
         ),
-        in_specs=[pl.BlockSpec(memory_space=pltpu.SMEM), vmem, vmem, vmem, vmem],
+        in_specs=[pl.BlockSpec(memory_space=pltpu.SMEM), anywhere, vmem, vmem, anywhere],
         out_specs=(vmem, vmem, anywhere),
         scratch_shapes=[
+            pltpu.VMEM((T, D), bf16),
+            pltpu.VMEM(own.shape, bf16),
             pltpu.VMEM((T, LANES), f32),
             pltpu.VMEM((D, T), bf16),
             pltpu.VMEM((O * F, G * T), bf16),
@@ -336,7 +348,7 @@
             pltpu.VMEM((2, T // 2, KV), f32),
             pltpu.VMEM((G, T, KV), bf16),
             pltpu.VMEM((G, T, KV), bf16),
-            dma((2,)), dma((R,)), dma((R,)), dma((5,)), dma((5,)),
+            dma((4,)), dma((R,)), dma((R,)), dma((5,)), dma((5,)),
             dma((2, O)), dma((2, O)), dma((O, G)), dma((O, G)),
             dma((6,)), dma((6,)), dma((O,)), dma((2, O)),
         ],
@@ -344,7 +356,7 @@
             collective_id=0, has_side_effects=True, vmem_limit_bytes=56 * 1024 * 1024
         ),
         cost_estimate=pl.CostEstimate(flops=4 * T * D * KV, bytes_accessed=16 * 1024 * 1024, transcendentals=T),
-    )(layer_index, inputs, norm_gain[None, :], cotangent, own)
+    )(layer_index, inputs, norm_gain, cotangent, own)
     weight_grad = grad[None]
     total = global_fragment - fragments[0].astype(f32)
     for k in range(1, R):

time: 90.2 us -> 84.8 us (0.940)
  Pallas kernels: 77.8 us -> 73.4 us
  local copies, waits for them, and re-layouts: 3.17 us -> 1.82 us
    pallas_call x1, Pallas kernels: 77.8 us -> 73.4 us  [body(): pl.pallas_call(functools.partial(kernel, R, G, O), out_shape=(jax.ShapeDt...]
    broadcast_in_dim x1 -> x0, local copies, waits for them, and re-layouts: 1.35 us -> none  [body(): norm_gain[None, :]]
where the time goes in v3:
time: 84.8 us; the launch traced here: 83.9 us
  Pallas kernels  73.4 us (87%)
  other arithmetic  7.41 us (9%)
  local copies, waits for them, and re-layouts  1.82 us (2%)
  between operations  1.32 us (2%)
    pallas_call x1, Pallas kernels, body(): pl.pallas_call(functools.partial(kernel, R, G, O), out_shape=(jax.ShapeDt...  73.4 us
    sub x1, other arithmetic, body(): new_global = global_fragment - 0.7 * (average + 0.9 * new_momentum)  7.41 us
    unnamed x8, local copies, waits for them, and re-layouts  1.82 us

profile of v3, /device:TPU:0, one launch (start us, length us, event | category | flops | bytes accessed | tf_op | source)
XLA Modules:
  0.0 83.9 jit_solution(3731558581388978741)
XLA Ops:
  1.3 0.0 copy-start
  1.3 73.4 %shard_map.102 = (bf16[256,1024]{1,0:T(8,128)(2,1)}, f32[288,1024]{1,0:T(8,128)}, bf16[2,4,288,1024]{3,2,1,0:T(8,128)(2,1)}) custom-call(s32[1]{0:T(128)S(6)} %copy.13.pick_ref, bf16[256,4608]{1,0:T(8,128)(2,1)} %x_hbm.1, f32[4608]{0:T(1024)} %gain_ref.1, bf16[256,1024]{1,0:T(8,128)(2,1)} %cot_ref.1, bf16[4,288,1024]{2,1,0:T(8,128)(2,1)} %bitcast.16), custom_call_target="tpu_custom_call" | custom-call | flops 4831838208 | bytes 16777216 | tf_op jit(solution)/shard_map/pallas_call | solution.py:327
  74.7 0.0 copy-done
  74.7 0.0 copy-start.2
  74.7 0.0 copy-start.1
  74.7 7.4 %multiply_subtract_fusion = (f32[4,288,1024]{2,1,0:T(8,128)}, f32[4,288,1024]{2,1,0:T(8,128)}) fusion(f32[4,288,1024]{2,1,0:T(8,128)S(1)} %copy-done, bf16[2,4,288,1024]{3,2,1,0:T(8,128)(2,1)} %get-tuple-element.9, f32[4,288,1024]{2,1,0:T(8,128)} %param.13), kind=kLoop, calls=%fused_computation.4 | loop fusion | flops 14155776 | bytes 23592960 | tf_op jit(solution)/shard_map/sub | solution.py:366
  82.1 0.0 copy-done.2
  82.1 0.8 copy.14
  82.9 0.0 copy-done.1
  82.9 1.0 %copy.15 = f32[1,288,1024]{2,1,0:T(8,128)} copy(f32[1,288,1024]{2,1,0:T(8,128)S(1)} %bitcast.15) | data formatting | bytes 2359296
Async XLA Ops:
  1.3 73.4 %copy-start = (f32[4,288,1024]{2,1,0:T(8,128)S(1)}, f32[4,288,1024]{2,1,0:T(8,128)}, u32[]{:S(2)}) copy-start(f32[4,288,1024]{2,1,0:T(8,128)} %param.12) | copy-start | bytes 14155780
  74.7 7.4 %copy-start.2 = (bf16[256,1024]{1,0:T(8,128)(2,1)S(1)}, bf16[256,1024]{1,0:T(8,128)(2,1)}, u32[]{:S(2)}) copy-start(bf16[256,1024]{1,0:T(8,128)(2,1)} %get-tuple-element.16) | copy-start | bytes 1572868
  74.7 8.2 %copy-start.1 = (f32[288,1024]{1,0:T(8,128)S(1)}, f32[288,1024]{1,0:T(8,128)}, u32[]{:S(2)}) copy-start(f32[288,1024]{1,0:T(8,128)} %get-tuple-element.8) | copy-start | bytes 3538948

commit v4 on v3

--- a/solution.py
+++ b/solution.py
@@ -171,16 +171,19 @@
     for k in range(1, R):
         frag_copy(k).start()
 
-    def sum_copy(d):
+    tile = KV // 2
+    halves = [pl.ds(m * tile, tile) for m in range(2)]
+
+    def sum_copy(d, m):
         side = jnp.where(z < d, 0, 1)
         return remote(
-            out_buf.at[d], in_buf.at[side, d], sum_s.at[d], sum_r.at[side, d],
+            out_buf.at[d, :, halves[m]], in_buf.at[side, d, :, halves[m]], sum_s.at[d, m], sum_r.at[side, d, m],
             at(r, jnp.where(z < d, z + 1, z - 1), c),
         )
 
-    def sum_wait(side, d):
-        where = in_buf.at[side, d]
-        remote(where, where, sum_s.at[d], sum_r.at[side, d], at(r, z, plane[1])).wait_recv()
+    def sum_wait(side, d, m):
+        where = in_buf.at[side, d, :, halves[m]]
+        remote(where, where, sum_s.at[d, m], sum_r.at[side, d, m], at(r, z, plane[1])).wait_recv()
 
     def pass_on(d):
         between = jnp.logical_and(d != z, jnp.logical_and(z > 0, z < O - 1))
@@ -188,11 +191,12 @@
         @pl.when(between)
         def _():
             side = jnp.where(z < d, 0, 1)
-            sum_wait(side, d)
-            out_buf[d] = (part[d] + in_buf[side, d].astype(jnp.float32)).astype(jnp.bfloat16)
-            sum_copy(d).start()
-
-    tile = min(512, KV)
+            for m, cols in enumerate(halves):
+                sum_wait(side, d, m)
+                got = in_buf[side, d, :, cols].astype(jnp.float32)
+                out_buf[d, :, cols] = (part[d, :, cols] + got).astype(jnp.bfloat16)
+                sum_copy(d, m).start()
+
     for n in range(O):
         d = order(n)
         if n and n + 1 < O:
@@ -206,15 +210,14 @@
                 cot_passed(k).wait_recv()
         for k in range(1, G):
             norm_copy(d, k).wait_recv()
-        for m in range(KV // tile):
-            cols = pl.ds(m * tile, tile)
+        first = jnp.logical_or(jnp.logical_and(z == 0, d > 0), jnp.logical_and(z == O - 1, d < O - 1))
+        for m, cols in enumerate(halves):
             part[d, :, cols] = jnp.dot(a[rows(d, F), :], cots[:, cols], preferred_element_type=jnp.float32)
-        first = jnp.logical_or(jnp.logical_and(z == 0, d > 0), jnp.logical_and(z == O - 1, d < O - 1))
-
-        @pl.when(first)
-        def _(d=d):
-            out_buf[d] = part[d].astype(jnp.bfloat16)
-            sum_copy(d).start()
+
+            @pl.when(first)
+            def _(d=d, m=m, cols=cols):
+                out_buf[d, :, cols] = part[d, :, cols].astype(jnp.bfloat16)
+                sum_copy(d, m).start()
 
         if n == O - 2:
             pass_on(order(0))
@@ -277,12 +280,14 @@
 
     @pl.when(has_left)
     def _():
-        sum_wait(0, z)
+        for m in range(2):
+            sum_wait(0, z, m)
         grad_ref[...] += in_buf[0, z].astype(jnp.float32)
 
     @pl.when(has_right)
     def _():
-        sum_wait(1, z)
+        for m in range(2):
+            sum_wait(1, z, m)
         grad_ref[...] += in_buf[1, z].astype(jnp.float32)
 
     grad_ref[...] = grad_ref[...] * scale
@@ -305,7 +310,8 @@
 
         @pl.when(z != d)
         def _(d=d):
-            sum_copy(d).wait_send()
+            for m in range(2):
+                sum_copy(d, m).wait_send()
     for hop in range(1, O):
         for side in range(2):
             @pl.when(w_sends(side, hop))
@@ -350,10 +356,10 @@
             pltpu.VMEM((G, T, KV), bf16),
             dma((4,)), dma((R,)), dma((R,)), dma((5,)), dma((5,)),
             dma((2, O)), dma((2, O)), dma((O, G)), dma((O, G)),
-            dma((6,)), dma((6,)), dma((O,)), dma((2, O)),
+            dma((6,)), dma((6,)), dma((O, 2)), dma((2, O, 2)),
         ],
         compiler_params=pltpu.CompilerParams(
-            collective_id=0, has_side_effects=True, vmem_limit_bytes=56 * 1024 * 1024
+            collective_id=0, has_side_effects=True, vmem_limit_bytes=40 * 1024 * 1024
         ),
         cost_estimate=pl.CostEstimate(flops=4 * T * D * KV, bytes_accessed=16 * 1024 * 1024, transcendentals=T),
     )(layer_index, inputs, norm_gain, cotangent, own)

time: 84.8 us -> 84.4 us (level)
  local copies, waits for them, and re-layouts: 1.82 us -> 6.9 us
  other arithmetic: 7.41 us -> 4.67 us
  Pallas kernels: 73.4 us -> 71.1 us
    unnamed x8 -> x14, local copies, waits for them, and re-layouts: 1.82 us -> 6.9 us
    sub x1, other arithmetic: 7.41 us -> 4.67 us  [body(): new_global = global_fragment - 0.7 * (average + 0.9 * new_momentum)]
    pallas_call x1, Pallas kernels: 73.4 us -> 71.1 us  [body(): pl.pallas_call(functools.partial(kernel, R, G, O), out_shape=(jax.ShapeDt...]
where the time goes in v4:
time: 84.4 us; the launch traced here: 84 us
  Pallas kernels  71.1 us (84%)
  local copies, waits for them, and re-layouts  6.9 us (8%)
  other arithmetic  4.67 us (6%)
  between operations  1.32 us (2%)
    pallas_call x1, Pallas kernels, body(): pl.pallas_call(functools.partial(kernel, R, G, O), out_shape=(jax.ShapeDt...  71.1 us
    unnamed x14, local copies, waits for them, and re-layouts  6.9 us
    sub x1, other arithmetic, body(): new_global = global_fragment - 0.7 * (average + 0.9 * new_momentum)  4.67 us

profile of v4, /device:TPU:0, one launch (start us, length us, event | category | flops | bytes accessed | tf_op | source)
XLA Modules:
  0.0 84.0 jit_solution(4590495530767524408)
XLA Ops:
  1.3 0.0 copy-start
  1.3 1.7 %copy-done = bf16[256,4608]{1,0:T(8,128)(2,1)S(1)} copy-done((bf16[256,4608]{1,0:T(8,128)(2,1)S(1)}, bf16[256,4608]{1,0:T(8,128)(2,1)}, u32[]{:S(2)}) %copy-start) | copy-done | bytes 2359320
  2.9 0.0 copy-start.1
  2.9 1.7 %copy-done.1 = bf16[1,4,288,1024]{3,2,1,0:T(8,128)(2,1)S(1)} copy-done((bf16[1,4,288,1024]{3,2,1,0:T(8,128)(2,1)S(1)}, bf16[1,4,288,1024]{3,2,1,0:T(8,128)(2,1)}, u32[]{:S(2)}) %copy-start.1) | copy-done | bytes 2359320
  4.6 0.0 copy-start.2
  4.6 1.0 %copy-done.2 = bf16[256,1024]{1,0:T(8,128)(2,1)S(1)} copy-done((bf16[256,1024]{1,0:T(8,128)(2,1)S(1)}, bf16[256,1024]{1,0:T(8,128)(2,1)}, u32[]{:S(2)}) %copy-start.2) | copy-done | bytes 524312
  5.7 0.0 copy-start.3
  5.7 0.7 copy-done.3
  6.4 0.0 copy-start.4
  6.4 0.0 copy-start.5
  6.4 71.1 %shard_map.102 = (bf16[256,1024]{1,0:T(8,128)(2,1)S(1)}, f32[288,1024]{1,0:T(8,128)S(1)}, bf16[2,4,288,1024]{3,2,1,0:T(8,128)(2,1)S(1)}) custom-call(s32[1]{0:T(128)S(6)} %copy.13.pick_ref, bf16[256,4608]{1,0:T(8,128)(2,1)S(1)} %copy-done, f32[4608]{0:T(1024)S(1)} %copy-done.3, bf16[256,1024]{1,0:T(8,128)(2,1)S(1)} %copy-done.2, ...), custom_call_target="tpu_custom_call" | custom-call | flops 4831838208 | bytes 16777216 | tf_op jit(solution)/shard_map/pallas_call | solution.py:333
  77.5 0.0 copy-done.4
  77.5 0.0 copy-done.5
  77.5 4.7 %multiply_subtract_fusion = (f32[4,288,1024]{2,1,0:T(8,128)}, f32[4,288,1024]{2,1,0:T(8,128)}) fusion(f32[4,288,1024]{2,1,0:T(8,128)S(1)} %copy-done.4, bf16[2,4,288,1024]{3,2,1,0:T(8,128)(2,1)S(1)} %get-tuple-element.9, f32[4,288,1024]{2,1,0:T(8,128)S(1)} %copy-done.5), kind=kLoop, calls=%fused_computation.4 | loop fusion | flops 14155776 | bytes 23592960 | tf_op jit(solution)/shard_map/sub | solution.py:372
  82.2 0.8 copy.14
  83.0 1.0 %copy.15 = f32[1,288,1024]{2,1,0:T(8,128)} copy(f32[1,288,1024]{2,1,0:T(8,128)S(1)} %bitcast.15) | data formatting | bytes 2359296
Async XLA Ops:
  1.3 1.7 %copy-start = (bf16[256,4608]{1,0:T(8,128)(2,1)S(1)}, bf16[256,4608]{1,0:T(8,128)(2,1)}, u32[]{:S(2)}) copy-start(bf16[256,4608]{1,0:T(8,128)(2,1)} %x_hbm.1) | copy-start | bytes 7077892
  2.9 1.7 %copy-start.1 = (bf16[1,4,288,1024]{3,2,1,0:T(8,128)(2,1)S(1)}, bf16[1,4,288,1024]{3,2,1,0:T(8,128)(2,1)}, u32[]{:S(2)}) copy-start(bf16[1,4,288,1024]{3,2,1,0:T(8,128)(2,1)} %param.11) | copy-start | bytes 7077892
  4.6 1.0 %copy-start.2 = (bf16[256,1024]{1,0:T(8,128)(2,1)S(1)}, bf16[256,1024]{1,0:T(8,128)(2,1)}, u32[]{:S(2)}) copy-start(bf16[256,1024]{1,0:T(8,128)(2,1)} %cot_ref.1) | copy-start | bytes 1572868
  5.7 0.7 copy-start.3
  6.4 71.1 %copy-start.4 = (f32[4,288,1024]{2,1,0:T(8,128)S(1)}, f32[4,288,1024]{2,1,0:T(8,128)}, u32[]{:S(2)}) copy-start(f32[4,288,1024]{2,1,0:T(8,128)} %param.12) | copy-start | bytes 14155780
  6.4 71.1 %copy-start.5 = (f32[4,288,1024]{2,1,0:T(8,128)S(1)}, f32[4,288,1024]{2,1,0:T(8,128)}, u32[]{:S(2)}) copy-start(f32[4,288,1024]{2,1,0:T(8,128)} %param.13) | copy-start | bytes 14155780

commit v5 on v4

--- a/solution.py
+++ b/solution.py
@@ -359,7 +359,7 @@
             dma((6,)), dma((6,)), dma((O, 2)), dma((2, O, 2)),
         ],
         compiler_params=pltpu.CompilerParams(
-            collective_id=0, has_side_effects=True, vmem_limit_bytes=40 * 1024 * 1024
+            collective_id=0, has_side_effects=True, vmem_limit_bytes=50 * 1024 * 1024
         ),
         cost_estimate=pl.CostEstimate(flops=4 * T * D * KV, bytes_accessed=16 * 1024 * 1024, transcendentals=T),
     )(layer_index, inputs, norm_gain, cotangent, own)

time: 84.4 us -> 83 us (0.983)
  local copies, waits for them, and re-layouts: 6.9 us -> 3.57 us
  other arithmetic: 4.67 us -> 6.54 us
    unnamed x14 -> x10, local copies, waits for them, and re-layouts: 6.9 us -> 3.57 us
    sub x1, other arithmetic: 4.67 us -> 6.54 us  [body(): new_global = global_fragment - 0.7 * (average + 0.9 * new_momentum)]
where the time goes in v5:
time: 83 us; the launch traced here: 82.2 us
  Pallas kernels  70.8 us (85%)
  other arithmetic  6.54 us (8%)
  local copies, waits for them, and re-layouts  3.57 us (4%)
  between operations  1.31 us (2%)
    pallas_call x1, Pallas kernels, body(): pl.pallas_call(functools.partial(kernel, R, G, O), out_shape=(jax.ShapeDt...  70.8 us
    sub x1, other arithmetic, body(): new_global = global_fragment - 0.7 * (average + 0.9 * new_momentum)  6.54 us
    unnamed x10, local copies, waits for them, and re-layouts  3.57 us

profile of v5, /device:TPU:0, one launch (start us, length us, event | category | flops | bytes accessed | tf_op | source)
XLA Modules:
  0.0 82.2 jit_solution(881069953832189135)
XLA Ops:
  1.3 0.0 copy-start
  1.3 1.0 %copy-done = bf16[256,1024]{1,0:T(8,128)(2,1)S(1)} copy-done((bf16[256,1024]{1,0:T(8,128)(2,1)S(1)}, bf16[256,1024]{1,0:T(8,128)(2,1)}, u32[]{:S(2)}) %copy-start) | copy-done | bytes 524312
  2.3 0.0 copy-start.1
  2.3 0.7 copy-done.1
  3.0 0.0 copy-start.2
  3.1 0.0 copy-start.3
  3.1 70.8 %shard_map.102 = (bf16[256,1024]{1,0:T(8,128)(2,1)S(1)}, f32[288,1024]{1,0:T(8,128)S(1)}, bf16[2,4,288,1024]{3,2,1,0:T(8,128)(2,1)}) custom-call(s32[1]{0:T(128)S(6)} %copy.13.pick_ref, bf16[256,4608]{1,0:T(8,128)(2,1)} %x_hbm.1, f32[4608]{0:T(1024)S(1)} %copy-done.1, bf16[256,1024]{1,0:T(8,128)(2,1)S(1)} %copy-done, bf16[4,288,1024]{2,1,0:T(8,128)(2,1)} %bitcast.16), custom_call_target="tpu_custom_call" | custom-call | flops 4831838208 | bytes 16777216 | tf_op jit(solution)/shard_map/pallas_call | solution.py:333
  73.8 0.0 copy-done.2
  73.8 0.0 copy-done.3
  73.8 6.5 %multiply_subtract_fusion = (f32[4,288,1024]{2,1,0:T(8,128)}, f32[4,288,1024]{2,1,0:T(8,128)}) fusion(f32[4,288,1024]{2,1,0:T(8,128)S(1)} %copy-done.2, bf16[2,4,288,1024]{3,2,1,0:T(8,128)(2,1)} %get-tuple-element.9, f32[4,288,1024]{2,1,0:T(8,128)S(1)} %copy-done.3), kind=kLoop, calls=%fused_computation.4 | loop fusion | flops 14155776 | bytes 23592960 | tf_op jit(solution)/shard_map/sub | solution.py:372
  80.4 0.8 copy.14
  81.2 1.0 %copy.15 = f32[1,288,1024]{2,1,0:T(8,128)} copy(f32[1,288,1024]{2,1,0:T(8,128)S(1)} %bitcast.15) | data formatting | bytes 2359296
Async XLA Ops:
  1.3 1.0 %copy-start = (bf16[256,1024]{1,0:T(8,128)(2,1)S(1)}, bf16[256,1024]{1,0:T(8,128)(2,1)}, u32[]{:S(2)}) copy-start(bf16[256,1024]{1,0:T(8,128)(2,1)} %cot_ref.1) | copy-start | bytes 1572868
  2.3 0.7 copy-start.1
  3.0 70.8 %copy-start.2 = (f32[4,288,1024]{2,1,0:T(8,128)S(1)}, f32[4,288,1024]{2,1,0:T(8,128)}, u32[]{:S(2)}) copy-start(f32[4,288,1024]{2,1,0:T(8,128)} %param.12) | copy-start | bytes 14155780
  3.1 70.8 %copy-start.3 = (f32[4,288,1024]{2,1,0:T(8,128)S(1)}, f32[4,288,1024]{2,1,0:T(8,128)}, u32[]{:S(2)}) copy-start(f32[4,288,1024]{2,1,0:T(8,128)} %param.13) | copy-start | bytes 14155780
